TPU v7x, 256 devices: a whole 4x4x8 slice. The times are simulated.
256 devices in a mesh: row: 32 (over y, x, core), frame: 8 (over z).
Axes of the slice: x: 4, y: 4, z: 8, core: 2. Of those that a mesh axis runs over, the one named last changes fastest.
Arguments:
- snapshots: float32 [65536, 8192], P('row', 'frame'), may hold values from -150 to 150
- test_matrix: float32 [8192, 256], P('frame'), may hold values from -0.0625 to 0.0625
Outputs:
- basis: float32 [65536, 256], P('row')
- coefficients: float32 [256, 8192], P(None, 'frame')
All inputs are finite; a program needn't handle non-finite values.
Results may differ from a plain program's by a relative error of at most 0.00014.
Values sent between devices are 32-bit elements; how exact they have to be, the bound alone decides.
A program may use at most 64 MiB of HBM per device.

v0:
```python
import jax
import jax.numpy as jnp
from jax import lax
from jax.sharding import PartitionSpec as P


def product(left, right):
    return jnp.dot(left, right, precision=lax.Precision.HIGHEST, preferred_element_type=jnp.float32)


def inner(left, right):
    return lax.dot_general(
        left,
        right,
        (((0,), (0,)), ((), ())),
        precision=lax.Precision.HIGHEST,
        preferred_element_type=jnp.float32,
    )


def on_device(snapshots, test_matrix):
    partial_sketch = product(snapshots, test_matrix)
    sketch = lax.psum(partial_sketch, "frame")
    gram = lax.psum(inner(sketch, sketch), "row")
    lower = jnp.linalg.cholesky(gram)
    basis_t = jax.scipy.linalg.solve_triangular(lower, sketch.T, lower=True)
    coefficients = lax.psum(product(basis_t, snapshots), "row")
    total_rows = sketch.shape[0] * lax.axis_size("row")
    basis = basis_t.T * jnp.sqrt(jnp.float32(total_rows))
    return (basis, coefficients)


def solution(mesh):
    placed = (P("row", "frame"), P("frame", None))
    return jax.shard_map(
        on_device,
        mesh=mesh,
        in_specs=placed,
        out_specs=(P("row", None), P(None, "frame")),
        check_vma=False,
    )
```

profile of v0, /device:TPU:1, one launch (start us, length us, event | category | flops | bytes accessed | tf_op | source)
XLA Modules:
  0.0 426.2 jit_solution(12882615674597149639)
XLA Ops:
  7.2 1.2 copy-done
  8.4 10.0 %fusion.11 = f32[2048,256]{1,0:T(8,128)} fusion(f32[2048,1024]{1,0:T(8,128)} %param.2, f32[1024,256]{1,0:T(8,128)S(1)} %copy-done), kind=kOutput, calls=%fused_computation.32 | convolution fusion | flops 6442450944 | bytes 11534336 | tf_op jit(solution)/shard_map/dot_general | solution.py:8
  18.5 82.7 %all-reduce.5.cloned.1.call-done = f32[2048,256]{1,0:T(8,128)} async-done(((f32[2048,256]{1,0:T(8,128)}), f32[2048,256]{1,0:T(8,128)}) %all-reduce.5.cloned.1.call-update) | async-done | bytes 2097168 | tf_op jit(solution)/shard_map/psum | solution.py:23
  101.2 6.4 %fusion.12 = f32[256,256]{0,1:T(8,128)} fusion(f32[2048,256]{1,0:T(8,128)} %all-reduce.5.cloned.1.call-done), kind=kOutput, calls=%fused_computation.33 | convolution fusion | flops 1610612736 | bytes 2359296 | tf_op jit(solution)/shard_map/dot_general | solution.py:12
  107.8 113.1 %all-reduce.7.cloned.1.call-done = f32[256,256]{0,1:T(8,128)} async-done(((f32[256,256]{0,1:T(8,128)}), f32[256,256]{0,1:T(8,128)}) %all-reduce.7.cloned.1.call-update) | async-done | bytes 262160 | tf_op jit(solution)/shard_map/psum | solution.py:24
  220.9 1.1 copy.5
  222.0 1.0 fusion.3
  223.7 11.7 %cholesky.50 = f32[128,128]{1,0:T(8,128)S(1)} custom-call(f32[128,128]{1,0:T(8,128)S(1)} %cholesky.118), custom_call_target="Cholesky" | custom-call | tf_op jit(solution)/shard_map/jit(cholesky)/cholesky | solution.py:25
  235.5 9.8 %custom-call.15 = f32[1,128,128]{1,2,0:T(8,128)S(1)} custom-call(f32[1,128,128]{2,1,0:T(8,128)S(1)} %get-tuple-element.25), custom_call_target="InvertDiagBlocksLowerTriangular" | custom-call | tf_op jit(solution)/shard_map/jit(cholesky)/cholesky | solution.py:25
  245.3 1.0 constant_dynamic-update-slice_fusion.1
  246.4 1.1 convolution_subtract_fusion.1
  247.5 11.7 %cholesky.105 = f32[128,128]{1,0:T(8,128)S(1)} custom-call(f32[128,128]{1,0:T(8,128)S(1)} %convolution_subtract_fusion.1), custom_call_target="Cholesky" | custom-call | tf_op jit(solution)/shard_map/jit(cholesky)/cholesky | solution.py:25
  262.2 5.3 %while.1 = (s32[]{:T(128)}, f32[256,256]{1,0:T(8,128)S(1)}, s32[2,2]{1,0:T(2,128)S(1)}, f32[2,128,128]{2,1,0:T(8,128)}, s32[]{:T(128)}) while((s32[]{:T(128)}, f32[256,256]{1,0:T(8,128)S(1)}, s32[2,2]{1,0:T(2,128)S(1)}, f32[2,128,128]{2,1,0:T(8,128)}, s32[]{:T(128)}) %tuple.28), condition=%wide.while_cond, body=%wide.while_body.sunk | while | flops 2 | bytes 132205 | solution.py:26
  263.0 2.0 bitcast_dynamic-update-slice_fusion.2
  265.6 2.0 bitcast_dynamic-update-slice_fusion.2
  267.5 20.5 %custom-call.16 = f32[2,128,128]{1,2,0:T(8,128)S(1)} custom-call(f32[2,128,128]{2,1,0:T(8,128)} %get-tuple-element.9), custom_call_target="InvertDiagBlocksLowerTriangular" | custom-call | tf_op jit(solution)/shard_map/jit(_solve_triangular)/triangular_solve | solution.py:26
  288.0 1.1 fusion.1
  289.1 1.8 convolution_subtract_fusion
  291.0 1.1 fusion.5
  292.0 10.4 %fusion = f32[256,1024]{1,0:T(8,128)} fusion(f32[2048,1024]{1,0:T(8,128)} %param.2, f32[128,2048]{1,0:T(8,128)S(1)} %fusion.5, f32[128,2048]{1,0:T(8,128)S(1)} %fusion.1), kind=kOutput, calls=%fused_computation.5 | convolution fusion | flops 6442975232 | bytes 11534336 | tf_op jit(solution)/shard_map/dot_general | solution.py:8
  302.5 2.7 multiply_bitcast_fusion
  305.2 2.9 copy.6
  308.1 109.2 %all-reduce.9.cloned.1.call-done = f32[256,1024]{1,0:T(8,128)} async-done(((f32[256,1024]{1,0:T(8,128)}), f32[256,1024]{1,0:T(8,128)}) %all-reduce.9.cloned.1.call-update) | async-done | bytes 1048592 | tf_op jit(solution)/shard_map/psum | solution.py:27
  417.4 2.3 copy.22
  (28 shorter events, 4.1 us)
Async XLA Ops:
  7.2 1.2 copy-start
  7.2 94.0 %all-reduce.5.cloned.1.call-start = ((), (), s32[]{:S(2)}) async-start(), calls=%async_computation | async-start | bytes 4194304 | tf_op jit(solution)/shard_map/psum | solution.py:23
  18.4 202.5 %all-reduce.7.cloned.1.call-start = ((), (), s32[]{:S(2)}) async-start(), calls=%async_computation.1 | async-start | bytes 524288 | tf_op jit(solution)/shard_map/psum | solution.py:24
  107.5 180.5 %copy-start.1 = (f32[2048,256]{1,0:T(8,128)S(1)}, f32[2048,256]{1,0:T(8,128)}, u32[]{:S(2)}) copy-start(f32[2048,256]{1,0:T(8,128)} %all-reduce.5.cloned.1.call-done) | copy-start | bytes 6291460
  107.6 309.8 %all-reduce.9.cloned.1.call-start = ((), (), s32[]{:S(2)}) async-start(), calls=%async_computation.2 | async-start | bytes 2097152 | tf_op jit(solution)/shard_map/psum | solution.py:27
  223.0 0.7 copy-start.4
  259.2 1.9 copy-start.3
  289.1 2.9 copy-start.2
Sparse Core Ops, SparseCore 0:
  18.5 82.5 all-reduce.4
  107.7 113.2 all-reduce.6
  302.6 114.7 all-reduce.8
where the time goes:
time: 427 us; the launch traced here: 426 us
  waiting for transfers between devices  305 us (71%)
  other arithmetic  59.2 us (14%)
  matrix products  32.9 us (8%)
  between operations  15.1 us (4%)
  local copies, waits for them, and re-layouts  13.4 us (3%)
    psum x1, waiting for transfers between devices, on_device(): gram = lax.psum(inner(sketch, sketch), 'row')  113 us
    psum x1, waiting for transfers between devices, on_device(): coefficients = lax.psum(product(basis_t, snapshots), 'row')  109 us
    psum x1, waiting for transfers between devices, on_device(): sketch = lax.psum(partial_sketch, 'frame')  82.7 us
    another operation x6, other arithmetic, on_device(): lower = jnp.linalg.cholesky(gram)  34 us
    another operation x3, other arithmetic, on_device(): basis_t = jax.scipy.linalg.solve_triangular(lower, sketch.T, lower=True)  21.5 us
    dot_general x2, matrix products, product(): jnp.dot(left, right, precision=lax.Precision.HIGHEST, preferred_element_t...  20.4 us
  transfers between devices with their start and end apart: 3, of which 3 were waited for; matrix products, arithmetic and copies ran while one was open for 1% of the time, Pallas kernels for 0%

commit v1 on v0

v1 whole, which is shorter than its diff:
```python
import functools

import jax
import jax.numpy as jnp
from jax import lax
from jax.experimental import pallas as pl
from jax.experimental.pallas import tpu as pltpu
from jax.sharding import PartitionSpec as P

HIGHEST = lax.Precision.HIGHEST
F32 = jnp.float32
BF16 = jnp.bfloat16
MESH = pl.DeviceIdType.MESH
NF = 8
NQ = 2


def split(x):
    high = x.astype(BF16)
    return high, (x - high.astype(F32)).astype(BF16)


def mm(a, b):
    return jnp.dot(a, b, preferred_element_type=F32)


def inner(a, b):
    return lax.dot_general(a, b, (((0,), (0,)), ((), ())), precision=HIGHEST, preferred_element_type=F32)


def at(i, size):
    return pl.ds(pl.multiple_of(i * size, size), size)


def iota(shape, dim):
    return lax.broadcasted_iota(jnp.int32, shape, dim)


def panel_start(p, g, ux, tmp, m):
    word = at(lax.div(p, 2), 128)
    odd = lax.rem(p, 2)
    tmp[...] = inner(ux[:, word], ux[...])
    took = tmp[at(odd, 64), :]
    eye = jnp.where(iota((64, 256), 0) + p * 64 == iota((64, 256), 1), 1.0, 0.0)
    tmp[0:64, 0:256] = g[at(p, 64), :] - took[:, 0:256]
    tmp[0:64, 256:512] = eye - took[:, 256:512]
    block = tmp[0:64, word]
    block = jnp.where(odd == 1, pltpu.roll(block, 64, 1), block)
    row, col = iota((64, 128), 0), iota((64, 128), 1)
    m[...] = jnp.where(col < 64, block, jnp.where(col - 64 == row, 1.0, 0.0))


def eliminate(m, t):
    sub = iota((8, 128), 0)
    lanes = lambda x, k: jnp.broadcast_to(x[:, k : k + 1], (8, 128))
    subl = lambda x, k: jnp.broadcast_to(x[k : k + 1, :], (8, 128))
    tile = m[at(t, 8), :]
    others = [m[8 * i : 8 * i + 8, :] for i in range(8)]
    cols = [lanes(tile, k) for k in range(8)]
    ocols = [[lanes(o, k) for k in range(8)] for o in others]
    pivots = jnp.ones((8, 128), F32)
    for k in range(8):
        row = subl(tile, k)
        pivot = subl(cols[k], k)
        inv = 1.0 / pivot
        pivots = jnp.where(sub == k, pivot, pivots)
        mult = jnp.where(sub > k, cols[k] * inv, 0.0)
        tile = tile - mult * row
        ahead = {j: subl(cols[j], k) for j in range(k + 1, 8)}
        for j in range(k + 1, 8):
            cols[j] = cols[j] - mult * ahead[j]
        for i in range(1, 8):
            mult_i = ocols[i][k] * inv
            others[i] = others[i] - mult_i * row
            for j in range(k + 1, 8):
                ocols[i][j] = ocols[i][j] - mult_i * ahead[j]
    for i in range(8):
        rows = slice(8 * i, 8 * i + 8)
        m[rows, :] = pltpu.roll(jnp.where(i > t, others[i], m[rows, :]), 120, 1)
    m[at(t, 8), :] = pltpu.roll(tile / jnp.sqrt(pivots), 120, 1)


def panel_end(p, ux, tmp, m):
    w = jnp.where(iota((64, 64), 1) <= iota((64, 64), 0), m[:, 0:64], 0.0)
    ux[at(p, 64), :] = jnp.dot(w, tmp[0:64, :], precision=HIGHEST, preferred_element_type=F32)


def cholesky_steps(first, last, g, ux, tmp, m):
    def step(s, carry):
        p, t = lax.div(s, 8), lax.rem(s, 8)

        @pl.when(t == 0)
        def _():
            panel_start(p, g, ux, tmp, m)

        eliminate(m, t)

        @pl.when(t == 7)
        def _():
            panel_end(p, ux, tmp, m)

        return carry

    lax.fori_loop(first, last, step, 0)


def main_kernel(
    nr, a_hbm, w_hbm, s_out, x_out, c_out,
    a, a_hi, a_lo, w, w_hi, w_lo, part, rs_buf, s_full,
    g_part, g_in, g_sum, gz, g, ux, tmp, m,
    c_part, c_pair, c_half, c_in, c_all,
    a_sem, w_sem, rs_s, rs_r, ag_s, ag_r, g1_s, g1_r, gz_s, gz_r, g2_s, g2_r,
    cp_s, cp_r, c1_s, c1_r, c2_s, c2_r, cf_s, cf_r, out_sem,
):
    row, z = lax.axis_index("row"), lax.axis_index("frame")
    right, left = lax.rem(z + 1, NF), lax.rem(z + NF - 1, NF)
    core, chip = lax.rem(row, 2), lax.div(row, 2)
    mate = row + 1 - 2 * core
    nc = nr // 2
    rb = part.shape[0] // NF
    hb = rb // 2
    ahead = lambda d: lax.rem(z + d + NF, NF)
    half = lambda block, h: pl.ds(pl.multiple_of(block * rb + h * hb, hb), hb)

    def to_z(src, dst, s, r, peer):
        return pltpu.make_async_remote_copy(src, dst, s, r, device_id={"frame": peer}, device_id_type=MESH)

    def to_row(src, dst, s, r, peer):
        return pltpu.make_async_remote_copy(src, dst, s, r, device_id={"row": peer}, device_id_type=MESH)

    barrier = pltpu.get_barrier_semaphore()

    def greet_row(k, carry):
        pl.semaphore_signal(barrier, inc=1, device_id={"row": lax.rem(row + k, nr)}, device_id_type=MESH)
        return carry

    def greet_z(k, carry):
        pl.semaphore_signal(barrier, inc=1, device_id={"frame": lax.rem(z + k, NF)}, device_id_type=MESH)
        return carry

    lax.fori_loop(1, NF, greet_z, 0)
    lax.fori_loop(1, nr, greet_row, 0)

    def units(i):
        d, h = lax.div(8 - i, 2), lax.rem(i, 2)
        return half(ahead(d), h), half(ahead(-d), 1 - h)

    def load(rows, side, i):
        return pltpu.make_async_copy(a_hbm.at[rows], a.at[rows], a_sem.at[side, i])

    pltpu.make_async_copy(w_hbm, w, w_sem).start()

    def fetch(i, carry):
        for side, rows in enumerate(units(i)):
            load(rows, side, i).start()
        return carry

    lax.fori_loop(0, 8, fetch, 0)
    pltpu.make_async_copy(w_hbm, w, w_sem).wait()
    w_hi[...], w_lo[...] = split(w[...])

    def sketch(rows):
        hi, lo = split(a[rows, :])
        a_hi[rows, :], a_lo[rows, :] = hi, lo
        part[rows, :] = mm(hi, w_hi[...]) + mm(lo, w_hi[...]) + mm(hi, w_lo[...])

    def rs_copy(side, i, rows):
        return to_z(part.at[rows], rs_buf.at[side, i], rs_s.at[side, i], rs_r.at[side, i], (right, left)[side])

    def rs_step(i, carry):
        rows = units(i)
        for side in range(2):
            load(rows[side], side, i).wait()
            sketch(rows[side])

        @pl.when(i == 0)
        def _():
            pl.semaphore_wait(barrier, nr - 1 + NF - 1)

        for side in range(2):
            @pl.when(i >= 2)
            def _():
                rs_copy(side, i - 2, rows[side]).wait_recv()
                part[rows[side], :] += rs_buf[side, i - 2]

            @pl.when(i < 7)
            def _():
                rs_copy(side, i, rows[side]).start()

        return carry

    lax.fori_loop(0, 8, rs_step, 0)
    for side in range(2):
        rows = half(z, side)
        rs_copy(side, 6, rows).wait_recv()
        part[rows, :] += rs_buf[side, 6]
    own = at(z, rb)
    kc = s_full.shape[2]
    for q in range(NQ):
        s_full[q, own, :] = part[own, q * kc : (q + 1) * kc]

    def ag_copy(side, n):
        q, j = lax.div(n, 7), lax.rem(n, 7)
        e, h = lax.div(j, 2), lax.rem(j, 2)
        rows = (half(ahead(-e), h), half(ahead(e), 1 - h))[side]
        ref = s_full.at[q, rows]
        return to_z(ref, ref, ag_s.at[side, n], ag_r.at[side, n], (right, left)[side])

    def ag_send(n):
        for side in range(2):
            if n % 7 >= 2:
                ag_copy(side, n - 2).wait_recv()
            ag_copy(side, n).start()

    def ag_land(n):
        for side in range(2):
            ag_copy(side, n).wait_recv()

    ag_send(0)
    ag_send(1)

    mine = part[own, :]
    g_part[...] = inner(mine, mine)

    def g1(k):
        peer = lax.rem(row + k, nr)
        return to_row(g_part.at[at(peer, 8)], g_in.at[k], g1_s.at[k], g1_r.at[k], peer)

    def g2(k):
        piece = g.at[at(row, 8)]
        return to_row(piece, piece, g2_s.at[k], g2_r.at[k], lax.rem(row + k, nr))

    def gzc(k):
        return to_z(g_sum, gz.at[z], gz_s.at[k], gz_r.at[k], lax.rem(z + k, NF))

    def loop(first, last, f):
        def body(k, carry):
            f(k)
            return carry

        lax.fori_loop(first, last, body, 0)

    loop(1, nr, lambda k: g1(k).start())

    def project(block, q):
        rows = at(block, rb)
        hi, lo = split(s_full[q, rows, :].T)
        both = mm(jnp.concatenate([hi, lo], 0), a_hi[rows, :])
        return both[:kc] + both[kc:] + mm(hi, a_lo[rows, :])

    def add_block(d, q):
        block = ahead(d)
        if d == 0:
            c_part[q] = project(block, q)
        else:
            c_part[q] += project(block, q)

    add_block(0, 0)
    ag_send(2)
    add_block(0, 1)
    loop(1, nr, lambda k: g1(k).wait_recv())
    total = g_part[at(row, 8), :]
    for k in range(1, nr):
        total = total + g_in[k]
    g_sum[...] = total
    gz[z] = total
    loop(1, NF, lambda k: gzc(k).start())
    ag_send(3)
    add_block(-1, 0)
    add_block(1, 0)
    ag_send(4)
    loop(1, NF, lambda k: gzc(k).wait_recv())
    total = gz[0]
    for k in range(1, NF):
        total = total + gz[k]
    g[at(row, 8), :] = total
    loop(1, nr, lambda k: g2(k).start())
    ag_send(5)
    ux[...] = jnp.zeros_like(ux)
    add_block(-2, 0)
    add_block(2, 0)
    ag_send(6)
    ag_send(7)
    ag_send(8)
    loop(1, nr, lambda k: g2(k).wait_recv())

    kh = kc // 2
    wide = c_half.shape[3]

    def pair(q):
        return to_row(c_part.at[q, at(1 - core, kh)], c_pair.at[q], cp_s.at[q], cp_r.at[q], mate)

    def c1(q, k):
        peer = lax.rem(chip + k, nc)
        return to_row(c_half.at[q, peer], c_in.at[q, k], c1_s.at[q, k], c1_r.at[q, k], peer * 2 + core)

    def c2(q, k):
        piece = c_all.at[q, core, chip]
        return to_row(piece, piece, c2_s.at[q, k], c2_r.at[q, k], lax.rem(chip + k, nc) * 2 + core)

    def back(q):
        ref = c_all.at[q, core]
        return to_row(ref, ref, cf_s.at[q], cf_r.at[q], mate)

    def c_scatter(q):
        pair(q).wait_recv()
        held = c_part[q, at(core, kh), :] + c_pair[q]
        for i in range(nc):
            r, l = divmod(i, nc // (kh // 8))
            c_half[q, i] = held[8 * r : 8 * r + 8, l * wide : (l + 1) * wide]
        loop(1, nc, lambda k: c1(q, k).start())

    def c_gather(q):
        loop(1, nc, lambda k: c1(q, k).wait_recv())
        total = c_half[q, chip]
        for k in range(1, nc):
            total = total + c_in[q, k]
        c_all[q, core, chip] = total
        loop(1, nc, lambda k: c2(q, k).start())

    def c_back(q):
        loop(1, nc, lambda k: c2(q, k).wait_recv())
        back(q).start()

    chol = functools.partial(cholesky_steps, g=g, ux=ux, tmp=tmp, m=m)
    chol(0, 2)
    ag_land(5)
    add_block(-3, 0)
    add_block(3, 0)
    ag_send(9)
    ag_land(6)
    add_block(4, 0)
    pair(0).start()
    chol(2, 5)
    c_scatter(0)
    ag_send(10)
    add_block(-1, 1)
    add_block(1, 1)
    chol(5, 8)
    ag_send(11)
    chol(8, 11)
    ag_send(12)
    add_block(-2, 1)
    add_block(2, 1)
    c_gather(0)
    chol(11, 14)
    ag_send(13)
    chol(14, 20)
    c_back(0)
    ag_land(12)
    add_block(-3, 1)
    add_block(3, 1)
    ag_land(13)
    s_copy = pltpu.make_async_copy(s_full, s_out, out_sem.at[0])
    s_copy.start()
    add_block(4, 1)
    pair(1).start()
    chol(20, 23)
    c_scatter(1)
    chol(23, 28)
    c_gather(1)
    chol(28, 32)
    x_copy = pltpu.make_async_copy(ux.at[:, 256:512], x_out, out_sem.at[1])
    x_copy.start()
    c_back(1)
    for q in range(NQ):
        back(q).wait_recv()
    c_copy = pltpu.make_async_copy(c_all, c_out, out_sem.at[2])
    c_copy.start()

    def rs_done(i):
        rows = units(i)
        for side in range(2):
            rs_copy(side, i, rows[side]).wait_send()

    def ag_done(n):
        for side in range(2):
            ag_copy(side, n).wait_send()

    loop(0, 7, rs_done)
    loop(0, 7 * NQ, ag_done)
    loop(1, NF, lambda k: gzc(k).wait_send())
    loop(1, nr, lambda k: g1(k).wait_send())
    loop(1, nr, lambda k: g2(k).wait_send())
    for q in range(NQ):
        pair(q).wait_send()
        back(q).wait_send()
        loop(1, nc, lambda k: c1(q, k).wait_send())
        loop(1, nc, lambda k: c2(q, k).wait_send())
    s_copy.wait()
    x_copy.wait()
    c_copy.wait()


def main(snapshots, test_matrix, nr):
    rows, frames = snapshots.shape
    k = test_matrix.shape[1]
    rb, kc, nc = rows // NF, k // NQ, nr // 2
    wide = (kc // 2) * frames // nc // 8
    any_space = pl.BlockSpec(memory_space=pl.ANY)
    vm = lambda *shape: pltpu.VMEM(shape, F32)
    vb = lambda *shape: pltpu.VMEM(shape, BF16)
    sem = lambda *shape: pltpu.SemaphoreType.DMA(shape)
    return pl.pallas_call(
        functools.partial(main_kernel, nr),
        out_shape=(
            jax.ShapeDtypeStruct((NQ, rows, kc), F32),
            jax.ShapeDtypeStruct((k, k), F32),
            jax.ShapeDtypeStruct((NQ, 2, nc, 8, wide), F32),
        ),
        in_specs=[any_space] * 2,
        out_specs=[any_space] * 3,
        scratch_shapes=[
            vm(rows, frames), vb(rows, frames), vb(rows, frames),
            vm(frames, k), vb(frames, k), vb(frames, k),
            vm(rows, k), vm(2, 7, rb // 2, k), vm(NQ, rows, kc),
            vm(k, k), vm(nr, 8, k), vm(8, k), vm(NF, 8, k), vm(k, k),
            vm(k, 2 * k), vm(128, 2 * k), vm(64, 128),
            vm(NQ, kc, frames), vm(NQ, kc // 2, frames), vm(NQ, nc, 8, wide), vm(NQ, nc, 8, wide), vm(NQ, 2, nc, 8, wide),
            sem(2, 8), pltpu.SemaphoreType.DMA, sem(2, 7), sem(2, 7), sem(2, 7 * NQ), sem(2, 7 * NQ),
            sem(nr), sem(nr), sem(NF), sem(NF), sem(nr), sem(nr),
            sem(NQ), sem(NQ), sem(NQ, nc), sem(NQ, nc), sem(NQ, nc), sem(NQ, nc), sem(NQ), sem(NQ), sem(3),
        ],
        compiler_params=pltpu.CompilerParams(
            collective_id=0, has_side_effects=True, vmem_limit_bytes=50 * 1024 * 1024
        ),
        name="sketch_gram_projection",
    )(snapshots, test_matrix)


def finish_kernel(scale, s, x, c, basis, coef):
    x_hi, x_lo = split(x[...])
    outer = lambda a, b: lax.dot_general(a, b, (((1,), (1,)), ((), ())), preferred_element_type=F32)

    def rows_of(ref):
        return jnp.concatenate([ref[q] for q in range(NQ)], axis=1)

    hi, lo = split(rows_of(s))
    basis[...] = (outer(hi, x_hi) + outer(lo, x_hi) + outer(hi, x_lo)) * scale

    @pl.when(pl.program_id(0) == 0)
    def _():
        nq, two, nc, eight, wide = c.shape
        across = coef.shape[1] // wide
        lines = []
        for q in range(nq):
            for h in range(two):
                for r in range(nc // across):
                    lines.append(jnp.concatenate([c[q, h, r * across + l] for l in range(across)], axis=1))
        c_hi, c_lo = split(jnp.concatenate(lines, axis=0))
        coef[...] = mm(x_hi, c_hi) + mm(x_lo, c_hi) + mm(x_hi, c_lo)


def finish(s, x, c, frames, scale):
    nq, rows, kc = s.shape
    k = nq * kc
    steps = 4
    rb = rows // steps
    return pl.pallas_call(
        functools.partial(finish_kernel, scale),
        grid=(steps,),
        out_shape=(jax.ShapeDtypeStruct((rows, k), F32), jax.ShapeDtypeStruct((k, frames), F32)),
        in_specs=[
            pl.BlockSpec((nq, rb, kc), lambda i: (0, i, 0)),
            pl.BlockSpec((k, k), lambda i: (0, 0)),
            pl.BlockSpec(c.shape, lambda i: (0,) * 5),
        ],
        out_specs=[
            pl.BlockSpec((rb, k), lambda i: (i, 0)),
            pl.BlockSpec((k, frames), lambda i: (0, 0)),
        ],
        compiler_params=pltpu.CompilerParams(vmem_limit_bytes=32 * 1024 * 1024),
        name="basis_and_coefficients",
    )(s, x, c)


def on_device(nr, snapshots, test_matrix):
    s, x, c = main(snapshots, test_matrix, nr)
    scale = float((snapshots.shape[0] * nr) ** 0.5)
    return finish(s, x, c, snapshots.shape[1], scale)


def solution(mesh):
    return jax.shard_map(
        functools.partial(on_device, mesh.shape["row"]),
        mesh=mesh,
        in_specs=(P("row", "frame"), P("frame", None)),
        out_specs=(P("row", None), P(None, "frame")),
        check_vma=False,
    )
```

time: 427 us -> 93.6 us (0.22)
  waiting for transfers between devices: 305 us -> 0 us
  Pallas kernels: 0 us -> 90 us
  other arithmetic: 59.2 us -> 0 us
  matrix products: 32.9 us -> 0 us
  between operations: 15.1 us -> 0.65 us
  local copies, waits for them, and re-layouts: 13.4 us -> 2.8 us
    psum x3 -> x0, waiting for transfers between devices: 305 us -> none  [the longest x1 113 us: on_device(): gram = lax.psum(inner(sketch, sketch), 'row')]
    pallas_call x0 -> x2, Pallas kernels: none -> 90 us  [the longest x1 86.1 us: main(): pl.pallas_call(functools.partial(main_kernel, nr), out_shape=(jax.ShapeDt...]
    another operation x9 -> x0, other arithmetic: 55.4 us -> none  [the longest x6 34 us: on_device(): lower = jnp.linalg.cholesky(gram)]
    dot_general x3 -> x0, matrix products: 26.8 us -> none  [the longest x2 20.4 us: product(): jnp.dot(left, right, precision=lax.Precision.HIGHEST, preferred_element_t...]
    another operation x5 -> x0, matrix products: 6.11 us -> none  [the longest x3 3.95 us: on_device(): basis_t = jax.scipy.linalg.solve_triangular(lower, sketch.T, lower=True)]
    another operation x9 -> x0, local copies, waits for them, and re-layouts: 5.25 us -> none
    unnamed x12 -> x4, local copies, waits for them, and re-layouts: 7.07 us -> 2.8 us
  transfers between devices with their start and end apart: 3 -> 0, of which waited for: 3 -> 0; matrix products, arithmetic and copies ran while one was open for 1% -> 0% of each run, Pallas kernels for 0% -> 0%
where the time goes in v1:
time: 93.6 us; the launch traced here: 93.5 us
  Pallas kernels  90 us (96%)
  local copies, waits for them, and re-layouts  2.8 us (3%)
    pallas_call x1, Pallas kernels, main(): pl.pallas_call(functools.partial(main_kernel, nr), out_shape=(jax.ShapeDt...  86.1 us
    pallas_call x1, Pallas kernels, finish(): pl.pallas_call(functools.partial(finish_kernel, scale), grid=(steps,), ou...  3.9 us
    unnamed x4, local copies, waits for them, and re-layouts  2.8 us

profile of v1, /device:TPU:1, one launch (start us, length us, event | category | flops | bytes accessed | tf_op | source)
XLA Modules:
  0.0 93.5 jit_solution(10335664231061990015)
XLA Ops:
  0.6 0.0 copy-start.1
  0.6 1.2 %copy-done.1 = f32[1024,256]{1,0:T(8,128)S(1)} copy-done((f32[1024,256]{1,0:T(8,128)S(1)}, f32[1024,256]{1,0:T(8,128)}, u32[]{:S(2)}) %copy-start.1) | copy-done | bytes 1048600
  1.9 86.1 %sketch_gram_projection.1 = (f32[2,2048,128]{2,1,0:T(8,128)}, f32[256,256]{1,0:T(8,128)S(1)}, f32[2,2,16,8,512]{4,3,2,1,0:T(8,128)S(1)}) custom-call(f32[2048,1024]{1,0:T(8,128)} %a_hbm.1, f32[1024,256]{1,0:T(8,128)S(1)} %copy-done.1), custom_call_target="tpu_custom_call" | custom-call | tf_op jit(solution)/shard_map/sketch_gram_projection/pallas_call | solution.py:404
  88.0 0.0 copy-start
  88.0 1.6 %copy-done = f32[2,2048,128]{2,1,0:T(8,128)S(1)} copy-done((f32[2,2048,128]{2,1,0:T(8,128)S(1)}, f32[2,2048,128]{2,1,0:T(8,128)}, u32[]{:S(2)}) %copy-start) | copy-done | bytes 2097176
  89.6 3.9 %basis_and_coefficients.1 = (f32[2048,256]{1,0:T(8,128)}, f32[256,1024]{1,0:T(8,128)}) custom-call(f32[2,2048,128]{2,1,0:T(8,128)S(1)} %copy-done, f32[256,256]{1,0:T(8,128)S(1)} %get-tuple-element.6.x, f32[2,2,16,8,512]{4,3,2,1,0:T(8,128)S(1)} %get-tuple-element.7.c), custom_call_target="tpu_custom_call" | custom-call | tf_op jit(solution)/shard_map/basis_and_coefficients/pallas_call | solution.py:459
Async XLA Ops:
  0.6 1.2 %copy-start.1 = (f32[1024,256]{1,0:T(8,128)S(1)}, f32[1024,256]{1,0:T(8,128)}, u32[]{:S(2)}) copy-start(f32[1024,256]{1,0:T(8,128)} %w_hbm.1) | copy-start | bytes 3145732
  88.0 1.6 %copy-start = (f32[2,2048,128]{2,1,0:T(8,128)S(1)}, f32[2,2048,128]{2,1,0:T(8,128)}, u32[]{:S(2)}) copy-start(f32[2,2048,128]{2,1,0:T(8,128)} %get-tuple-element.5.s) | copy-start | bytes 6291460

commit v2 on v0

v2 whole, which is shorter than its diff:
```python
import functools

import jax
import jax.numpy as jnp
from jax import lax
from jax.experimental import pallas as pl
from jax.experimental.pallas import tpu as pltpu
from jax.sharding import PartitionSpec as P

HIGHEST = lax.Precision.HIGHEST
F32 = jnp.float32
BF16 = jnp.bfloat16
MESH = pl.DeviceIdType.MESH
NF = 8
CHUNKS = (128, 96, 32)

PLAN = (
    ("S", 0), ("N", 0), ("R", 0, 0), ("R", 1, 0), ("R", 2, 0), ("S", 1), ("R", 0, 1), ("R", 1, 1), ("R", 2, 1),
    ("S", 2), ("S", 3), ("S", 4), ("S", 5), ("S", 6), ("R", 0, 2), ("S", 7), ("R", 1, 2), ("R", 2, 2), ("N", 1),
    ("R", 0, 3), ("R", 1, 3), ("R", 2, 3), ("N", 2), ("R", 0, 4), ("R", 1, 4), ("R", 2, 4), ("N", 3), ("R", 0, 5),
    ("R", 1, 5), ("R", 2, 5), ("N", 4), ("R", 0, 6), ("R", 1, 6), ("R", 2, 6), ("R", 0, 7), ("R", 1, 7), ("R", 2, 7),
    ("R", 0, 8), ("A", 0, 0), ("A", 0, 1), ("P", 0, 0), ("R", 1, 8), ("A", 1, 0), ("A", 1, 1), ("P", 0, 1),
    ("R", 2, 8), ("G", 0), ("P", 0, 2), ("A", 0, 2), ("A", 0, 3), ("P", -1, 0), ("P", 1, 0), ("A", 1, 2), ("A", 2, 0),
    ("A", 1, 3), ("P", -1, 1), ("P", 1, 1), ("A", 0, 4), ("G", 1), ("A", 0, 5), ("A", 2, 1), ("P", -2, 0),
    ("P", 2, 0), ("A", 1, 4), ("A", 2, 2), ("A", 0, 6), ("A", 1, 5), ("P", -2, 1), ("P", 2, 1), ("A", 0, 7),
    ("P", -3, 0), ("A", 2, 3), ("G", 2), ("P", 3, 0), ("P", -1, 2), ("A", 1, 6), ("P", 1, 2), ("A", 2, 4),
    ("A", 0, 8), ("P", 4, 0), ("C", 0, 0), ("A", 1, 7), ("P", -3, 1), ("A", 2, 5), ("P", 3, 1), ("P", -2, 2),
    ("C", 0, 1), ("P", 2, 2), ("A", 1, 8), ("P", 4, 1), ("A", 2, 6), ("C", 1, 0), ("C", 1, 1), ("G", 3), ("A", 2, 7),
    ("P", -3, 2), ("P", 3, 2), ("H", 0, 0), ("A", 2, 8), ("P", 4, 2), ("C", 2, 0), ("H", 0, 1), ("C", 2, 1),
    ("H", 1, 0), ("C", 0, 2), ("H", 1, 1), ("C", 1, 2), ("H", 2, 0), ("H", 2, 1), ("C", 2, 2), ("H", 3, 0),
    ("H", 3, 1), ("B", 0), ("C", 0, 3), ("B", 1), ("B", 2), ("B", 3), ("B", 4), ("B", 5), ("B", 6), ("D", 0),
    ("C", 1, 3), ("B", 7), ("C", 2, 3), ("D", 1), ("D", 2),
)


def split(x):
    high = x.astype(BF16)
    return high, (x - high.astype(F32)).astype(BF16)


def mm(a, b):
    return jnp.dot(a, b, preferred_element_type=F32)


def inner(a, b):
    return lax.dot_general(a, b, (((0,), (0,)), ((), ())), precision=HIGHEST, preferred_element_type=F32)


def outer(a, b, precision=None):
    return lax.dot_general(a, b, (((1,), (1,)), ((), ())), precision=precision, preferred_element_type=F32)


def at(i, size):
    return pl.ds(pl.multiple_of(i * size, size), size)


def iota(shape, dim):
    return lax.broadcasted_iota(jnp.int32, shape, dim)


def panel_begin(p, g, ux, win, m):
    lo, hi = 64 * p, 64 * p + 64
    rows = g[lo:hi, :]
    if p:
        rows = jnp.concatenate([rows[:, lo:], jnp.zeros((64, lo), F32)], axis=1)
        rows = rows - inner(ux[0:lo, lo:hi], ux[0:lo, lo : lo + 256])
    win[...] = rows
    eye = jnp.where(iota((64, 64), 0) == iota((64, 64), 1), 1.0, 0.0)
    m[...] = jnp.concatenate([rows[:, 0:64], eye], axis=1)


def eliminate(m, groups):
    sub = iota((8, 128), 0)
    lanes = lambda x, k: jnp.broadcast_to(x[:, k : k + 1], (8, 128))
    subl = lambda x, k: jnp.broadcast_to(x[k : k + 1, :], (8, 128))
    tiles = {i: m[8 * i : 8 * i + 8, :] for i in range(groups[0], 8)}
    for t in groups:
        cols = {i: [lanes(tiles[i], 8 * t + k) for k in range(8)] for i in range(t, 8)}
        pivots = jnp.ones((8, 128), F32)
        for k in range(8):
            row = subl(tiles[t], k)
            pivot = subl(cols[t][k], k)
            inv = 1.0 / pivot
            pivots = jnp.where(sub == k, pivot, pivots)
            ahead = {j: subl(cols[t][j], k) for j in range(k + 1, 8)}
            for i in range(t, 8):
                mult = cols[i][k] * inv
                if i == t:
                    mult = jnp.where(sub > k, mult, 0.0)
                tiles[i] = tiles[i] - mult * row
                for j in range(k + 1, 8):
                    cols[i][j] = cols[i][j] - mult * ahead[j]
        m[8 * t : 8 * t + 8, :] = tiles[t] / jnp.sqrt(pivots)
    for i in range(groups[-1] + 1, 8):
        m[8 * i : 8 * i + 8, :] = tiles[i]


def panel_end(p, ux, win, m):
    lo, hi = 64 * p, 64 * p + 64
    w = jnp.where(iota((64, 64), 1) <= iota((64, 64), 0), m[:, 64:128], 0.0)
    ux[lo:hi, lo : lo + 256] = jnp.dot(w, win[...], precision=HIGHEST, preferred_element_type=F32)
    ux[lo:hi, 256 + lo : 256 + hi] = w


def cholesky_step(p, half, g, ux, win, m):
    if half == 0:
        panel_begin(p, g, ux, win, m)
    eliminate(m, range(4 * half, 4 * half + 4))
    if half == 1:
        panel_end(p, ux, win, m)


def main_kernel(nr, scale, *refs):
    a_hbm, w_hbm, b_out, x_out, c_out = refs[:5]
    a, a_hi, a_lo, w, w_hi, w_lo, part, rs_buf, st = refs[5:14]
    g_part, g_in, g_sum, gz, g, ux, win, m = refs[14:22]
    c_part, c_pair, c_half, c_in, c_all = refs[22:27]
    a_sem, w_sem, rs_s, rs_r, ag_s, ag_r, g1_s, g1_r, gz_s, gz_r, g2_s, g2_r = refs[27:39]
    cp_s, cp_r, c1_s, c1_r, c2_s, c2_r, cf_s, cf_r, out_sem, near = refs[39:]
    row, z = lax.axis_index("row"), lax.axis_index("frame")
    right, left = lax.rem(z + 1, NF), lax.rem(z + NF - 1, NF)
    core, chip = lax.rem(row, 2), lax.div(row, 2)
    mate = row + 1 - 2 * core
    nc = nr // 2
    hb = st.shape[2]
    frames = a.shape[1]
    across = frames // 128
    ahead = lambda d: lax.rem(z + d + NF, NF)
    rows_of = lambda u: at(u, hb)
    starts = [sum(CHUNKS[:c]) for c in range(len(CHUNKS))]
    span = [slice(starts[c], starts[c] + CHUNKS[c]) for c in range(len(CHUNKS))]
    cut = lambda c: pl.ds(starts[c], CHUNKS[c])
    tiles = [n * across // 16 // nc for n in CHUNKS]
    slots = [pl.ds(sum(tiles[:c]), tiles[c]) for c in range(len(CHUNKS))]

    def to_z(src, dst, s, r, peer):
        return pltpu.make_async_remote_copy(src, dst, s, r, device_id={"frame": peer}, device_id_type=MESH)

    def to_row(src, dst, s, r, peer):
        return pltpu.make_async_remote_copy(src, dst, s, r, device_id={"row": peer}, device_id_type=MESH)

    def loop(first, last, f):
        def body(k, carry):
            f(k)
            return carry

        lax.fori_loop(first, last, body, 0)

    barrier = pltpu.get_barrier_semaphore()
    nx = 4
    x, y, ny = lax.rem(chip, nx), lax.div(chip, nx), nc // nx
    at_chip = lambda yy, xx: {"row": (lax.rem(yy + ny, ny) * nx + lax.rem(xx + nx, nx)) * 2 + core}
    neighbours = ({"frame": right}, {"frame": left}, {"row": mate})
    neighbours += (at_chip(y, x + 1), at_chip(y, x - 1), at_chip(y + 1, x), at_chip(y - 1, x))

    def greet(which):
        for peer in neighbours:
            pl.semaphore_signal(which, inc=1, device_id=peer, device_id_type=MESH)

    def greeted(which):
        pl.semaphore_wait(which, len(neighbours))

    def meet(stage):
        if stage:
            greeted(near.at[stage - 1])
        else:
            greeted(barrier)
        if stage < 4:
            greet(near.at[stage])

    greet(barrier)

    def units(i):
        if isinstance(i, int):
            d, h = ((8 - i) // 2, i % 2) if i < 8 else (0, 0)
        else:
            d, h = lax.div(8 - i, 2), lax.rem(i, 2)
        return 2 * ahead(d) + h, 2 * ahead(-d) + 1 - h

    def load(u, side, i):
        return pltpu.make_async_copy(a_hbm.at[rows_of(u)], a.at[rows_of(u)], a_sem.at[side, i])

    w_copy = pltpu.make_async_copy(w_hbm, w, w_sem)

    def fetch(i):
        for side, u in enumerate(units(i)):
            load(u, side, i).start()

    w_copy.start()
    fetch(0)
    fetch(1)
    ux[:, 256:512] = jnp.zeros((ux.shape[0], 256), F32)
    w_copy.wait()
    fetch(2)
    w_hi[...], w_lo[...] = split(w[...])

    def sketch(i):
        if i + 3 < 8:
            fetch(i + 3)
        for side, u in enumerate(units(i)):
            load(u, side, i).wait()
            hi, lo = split(a[rows_of(u), :])
            a_hi[rows_of(u), :], a_lo[rows_of(u), :] = hi, lo
            part[u] = (mm(hi, w_hi[...]) + mm(lo, w_hi[...]) + mm(hi, w_lo[...])).T

    def rs_copy(side, c, i, u):
        dst = rs_buf.at[side, i, cut(c)]
        return to_z(part.at[u, cut(c)], dst, rs_s.at[side], rs_r.at[side, c, i], (right, left)[side])

    def reduce_step(c, i):
        for side, u in enumerate(units(i)):
            if i >= 2:
                rs_copy(side, c, i - 2, u).wait_recv()
                total = part[u, span[c]] + rs_buf[side, i - 2, span[c]]
                if i < 8:
                    part[u, span[c]] = total
                else:
                    st[u, span[c]] = total
            if i < 7:
                rs_copy(side, c, i, u).start()

    def ag_copy(side, c, j):
        e, h = (j // 2, j % 2) if isinstance(j, int) else (lax.div(j, 2), lax.rem(j, 2))
        u = (2 * ahead(-e) + h, 2 * ahead(e) + 1 - h)[side]
        ref = st.at[u, cut(c)]
        return to_z(ref, ref, ag_s.at[side], ag_r.at[side, c, j], (right, left)[side])

    def gather_step(c, j):
        for side in range(2):
            if j >= 2:
                ag_copy(side, c, j - 2).wait_recv()
            if j < 7:
                ag_copy(side, c, j).start()

    def g1(k):
        peer = lax.rem(row + k, nr)
        return to_row(g_part.at[at(peer, 8)], g_in.at[k], g1_s, g1_r, peer)

    def g2(k):
        piece = g.at[at(row, 8)]
        return to_row(piece, piece, g2_s, g2_r, lax.rem(row + k, nr))

    def gzc(k):
        return to_z(g_sum, gz.at[z], gz_s, gz_r, lax.rem(z + k, NF))

    def g1_all():
        ref = g_in.at[pl.ds(1, nr - 1)]
        return to_row(ref, ref, g1_s, g1_r, mate)

    def gz_all():
        ref = gz.at[pl.ds(1, NF - 1)]
        return to_z(ref, ref, gz_s, gz_r, right)

    def g2_all():
        ref = g.at[pl.ds(8, 8 * (nr - 1))]
        return to_row(ref, ref, g2_s, g2_r, mate)

    def c1_all(c):
        ref = c_in.at[pl.ds(1, nc - 1), slots[c]]
        return to_row(ref, ref, c1_s.at[c], c1_r.at[c], mate)

    def c2_all(c):
        ref = c_all.at[core, pl.ds(1, nc - 1), slots[c]]
        return to_row(ref, ref, c2_s.at[c], c2_r.at[c], mate)

    def gram_step(stage):
        if stage == 0:
            mine = jnp.concatenate([st[2 * z], st[2 * z + 1]], axis=1)
            g_part[...] = outer(mine, mine, HIGHEST)
            loop(1, nr, lambda k: g1(k).start())
        elif stage == 1:
            g1_all().wait_recv()
            total = g_part[at(row, 8), :]
            for k in range(1, nr):
                total = total + g_in[k]
            g_sum[...] = total
            gz[z] = total
            loop(1, NF, lambda k: gzc(k).start())
        elif stage == 2:
            gz_all().wait_recv()
            total = gz[0]
            for k in range(1, NF):
                total = total + gz[k]
            g[at(row, 8), :] = total
            loop(1, nr, lambda k: g2(k).start())
        else:
            g2_all().wait_recv()

    def project(d, c):
        block = ahead(d)
        kc = CHUNKS[c]
        rows = at(block, 2 * hb)
        hi, lo = split(jnp.concatenate([st[2 * block, span[c]], st[2 * block + 1, span[c]]], axis=1))
        both = mm(jnp.concatenate([hi, lo], 0), a_hi[rows, :])
        total = both[:kc] + both[kc:] + mm(hi, a_lo[rows, :])
        c_part[span[c], :] = total if d == 0 else c_part[span[c], :] + total

    def pair(c):
        kh = CHUNKS[c] // 2
        src = c_part.at[pl.ds(pl.multiple_of(starts[c] + (1 - core) * kh, 8), kh)]
        return to_row(src, c_pair.at[pl.ds(starts[c] // 2, kh)], cp_s.at[c], cp_r.at[c], mate)

    def c1(c, k):
        peer = lax.rem(chip + k, nc)
        return to_row(c_half.at[peer, slots[c]], c_in.at[k, slots[c]], c1_s.at[c], c1_r.at[c], peer * 2 + core)

    def c2(c, k):
        piece = c_all.at[core, chip, slots[c]]
        return to_row(piece, piece, c2_s.at[c], c2_r.at[c], lax.rem(chip + k, nc) * 2 + core)

    def back(c):
        ref = c_all.at[core, :, slots[c]]
        return to_row(ref, ref, cf_s.at[c], cf_r.at[c], mate)

    def plane_step(c, stage):
        kh = CHUNKS[c] // 2
        if stage == 0:
            pair(c).start()
        elif stage == 1:
            pair(c).wait_recv()
            mine = pl.ds(pl.multiple_of(starts[c] + core * kh, 8), kh)
            held = c_part[mine, :] + c_pair[starts[c] // 2 : starts[c] // 2 + kh]
            for t in range(kh // 8 * across):
                r, l = divmod(t, across)
                i, s = divmod(t, tiles[c])
                c_half[i, sum(tiles[:c]) + s] = held[8 * r : 8 * r + 8, 128 * l : 128 * l + 128]
            loop(1, nc, lambda k: c1(c, k).start())
        elif stage == 2:
            c1_all(c).wait_recv()
            total = c_half[chip, slots[c]]
            for k in range(1, nc):
                total = total + c_in[k, slots[c]]
            c_all[core, chip, slots[c]] = total
            loop(1, nc, lambda k: c2(c, k).start())
        else:
            c2_all(c).wait_recv()
            back(c).start()

    def c_copy(c, h):
        piece = (h, slice(None), slots[c])
        return pltpu.make_async_copy(c_all.at[piece], c_out.at[piece], out_sem.at[c])

    def c_land(c):
        back(c).wait_recv()
        for h in range(2):
            c_copy(c, h).start()

    x_copy = pltpu.make_async_copy(ux.at[:, 256:512], x_out, out_sem.at[len(CHUNKS)])
    held_x = []

    def b_copy(i):
        rows = pl.ds(2 * hb * i, 2 * hb)
        return pltpu.make_async_copy(a.at[rows, pl.ds(0, ux.shape[0])], b_out.at[rows], out_sem.at[len(CHUNKS) + 1 + i])

    def basis_step(i):
        if i == 0:
            x_copy.start()
            held_x.extend(split(ux[:, 256:512]))
        hi, lo = split(jnp.concatenate([st[2 * i].T, st[2 * i + 1].T], axis=0))
        block = outer(hi, held_x[0]) + outer(lo, held_x[0]) + outer(hi, held_x[1])
        a[2 * hb * i : 2 * hb * (i + 1), 0 : ux.shape[0]] = block * scale
        b_copy(i).start()

    steps = {
        "N": meet,
        "S": sketch,
        "R": reduce_step,
        "A": gather_step,
        "G": gram_step,
        "P": project,
        "C": plane_step,
        "D": c_land,
        "H": functools.partial(cholesky_step, g=g, ux=ux, win=win, m=m),
        "B": basis_step,
    }
    for name, *numbers in PLAN:
        steps[name](*numbers)

    for c in range(len(CHUNKS)):
        pair(c).wait_send()
        back(c).wait_send()
        c1_all(c).wait_send()
        c2_all(c).wait_send()
    for side in range(2):
        ref = rs_buf.at[side]
        to_z(ref, ref, rs_s.at[side], rs_r.at[side, 0, 0], right).wait_send()
        to_z(ref, ref, ag_s.at[side], ag_r.at[side, 0, 0], right).wait_send()
    gz_all().wait_send()
    g1_all().wait_send()
    g2_all().wait_send()
    x_copy.wait()
    for i in range(NF):
        b_copy(i).wait()
    for c in range(len(CHUNKS)):
        for h in range(2):
            c_copy(c, h).wait()


def main(snapshots, test_matrix, nr, scale):
    rows, frames = snapshots.shape
    k = test_matrix.shape[1]
    hb, nc, nq = rows // NF // 2, nr // 2, len(CHUNKS)
    tiles = k * (frames // 128) // 16 // nc
    hbm = pl.BlockSpec(memory_space=pltpu.HBM)
    vm = lambda *shape: pltpu.VMEM(shape, F32)
    vb = lambda *shape: pltpu.VMEM(shape, BF16)
    sem = lambda *shape: pltpu.SemaphoreType.DMA(shape)
    one = pltpu.SemaphoreType.DMA
    return pl.pallas_call(
        functools.partial(main_kernel, nr, scale),
        out_shape=(
            jax.ShapeDtypeStruct((rows, k), F32),
            jax.ShapeDtypeStruct((k, k), F32),
            jax.ShapeDtypeStruct((2, nc, tiles, 8, 128), F32),
        ),
        in_specs=[hbm] * 2,
        out_specs=[hbm] * 3,
        scratch_shapes=[
            vm(rows, frames), vb(rows, frames), vb(rows, frames),
            vm(frames, k), vb(frames, k), vb(frames, k),
            vm(2 * NF, k, hb), vm(2, 7, k, hb), vm(2 * NF, k, hb),
            vm(k, k), vm(nr, 8, k), vm(8, k), vm(NF, 8, k), vm(k, k),
            vm(k, 2 * k), vm(64, k), vm(64, 128),
            vm(k, frames), vm(k // 2, frames), vm(nc, tiles, 8, 128), vm(nc, tiles, 8, 128), vm(2, nc, tiles, 8, 128),
            sem(2, 8), one, sem(2), sem(2, nq, 7), sem(2), sem(2, nq, 7),
            one, one, one, one, one, one,
            sem(nq), sem(nq), sem(nq), sem(nq), sem(nq), sem(nq), sem(nq), sem(nq), sem(nq + 1 + NF),
            pltpu.SemaphoreType.REGULAR((4,)),
        ],
        compiler_params=pltpu.CompilerParams(
            collective_id=0, has_side_effects=True, vmem_limit_bytes=62 * 1024 * 1024
        ),
        name="sketch_gram_projection",
    )(snapshots, test_matrix)


def finish_kernel(b_hbm, x_hbm, c_hbm, basis_hbm, coef_hbm, b, x, c, coef, b_sem, s_sem, in_sem, f_sem):
    parts = b_sem.shape[0]
    per = b_hbm.shape[0] // parts
    loads = [pltpu.make_async_copy(x_hbm, x, in_sem.at[0]), pltpu.make_async_copy(c_hbm, c, in_sem.at[1])]
    passed, stores = [], []
    for i in range(parts):
        rows = pl.ds(i * per, per)
        passed.append(pltpu.make_async_copy(b_hbm.at[rows], b.at[rows], b_sem.at[i]))
        stores.append(pltpu.make_async_copy(b.at[rows], basis_hbm.at[rows], s_sem.at[i]))
    for copy in loads + passed:
        copy.start()
    for load, store in zip(passed, stores):
        load.wait()
        store.start()
    loads[0].wait()
    x_hi, x_lo = split(x[...])
    loads[-1].wait()
    _, nc, total, _, _ = c.shape
    across = coef.shape[1] // 128
    lines = [None] * (x.shape[0] // 8)
    for h in range(2):
        for q, n in enumerate(CHUNKS):
            first, tiles = sum(CHUNKS[:q]) * total // x.shape[0], n * total // x.shape[0]
            for r in range(n // 16):
                line = [divmod(r * across + l, tiles) for l in range(across)]
                place = (sum(CHUNKS[:q]) + h * n // 2) // 8 + r
                lines[place] = jnp.concatenate([c[h, i, first + t] for i, t in line], axis=1)
    c_hi, c_lo = split(jnp.concatenate(lines, axis=0))
    coef[...] = mm(x_hi, c_hi) + mm(x_lo, c_hi) + mm(x_hi, c_lo)
    stores.append(pltpu.make_async_copy(coef, coef_hbm, f_sem))
    stores[-1].start()
    for copy in stores:
        copy.wait()


def finish(b, x, c, frames):
    hbm = pl.BlockSpec(memory_space=pltpu.HBM)
    vm = lambda *shape: pltpu.VMEM(shape, F32)
    return pl.pallas_call(
        finish_kernel,
        out_shape=(jax.ShapeDtypeStruct(b.shape, F32), jax.ShapeDtypeStruct((x.shape[0], frames), F32)),
        in_specs=[hbm] * 3,
        out_specs=[hbm] * 2,
        scratch_shapes=[
            vm(*b.shape), vm(*x.shape), vm(*c.shape), vm(x.shape[0], frames),
            pltpu.SemaphoreType.DMA((4,)), pltpu.SemaphoreType.DMA((4,)), pltpu.SemaphoreType.DMA((2,)), pltpu.SemaphoreType.DMA,
        ],
        compiler_params=pltpu.CompilerParams(vmem_limit_bytes=62 * 1024 * 1024),
        name="coefficients",
    )(b, x, c)


def on_device(nr, snapshots, test_matrix):
    scale = float((snapshots.shape[0] * nr) ** 0.5)
    b, x, c = main(snapshots, test_matrix, nr, scale)
    return finish(b, x, c, snapshots.shape[1])


def solution(mesh):
    return jax.shard_map(
        functools.partial(on_device, mesh.shape["row"]),
        mesh=mesh,
        in_specs=(P("row", "frame"), P("frame", None)),
        out_specs=(P("row", None), P(None, "frame")),
        check_vma=False,
    )
```

time: 427 us -> 81 us (0.19)
  waiting for transfers between devices: 305 us -> 0 us
  Pallas kernels: 0 us -> 80.1 us
  other arithmetic: 59.2 us -> 0 us
  matrix products: 32.9 us -> 0 us
  between operations: 15.1 us -> 0.8 us
  local copies, waits for them, and re-layouts: 13.4 us -> 0 us
    psum x3 -> x0, waiting for transfers between devices: 305 us -> none  [the longest x1 113 us: on_device(): gram = lax.psum(inner(sketch, sketch), 'row')]
    pallas_call x0 -> x2, Pallas kernels: none -> 80.1 us  [the longest x1 76.5 us: main(): pl.pallas_call(functools.partial(main_kernel, nr, scale), out_shape=(jax....]
    another operation x9 -> x0, other arithmetic: 55.4 us -> none  [the longest x6 34 us: on_device(): lower = jnp.linalg.cholesky(gram)]
    dot_general x3 -> x0, matrix products: 26.8 us -> none  [the longest x2 20.4 us: product(): jnp.dot(left, right, precision=lax.Precision.HIGHEST, preferred_element_t...]
    unnamed x12 -> x0, local copies, waits for them, and re-layouts: 7.07 us -> none
    another operation x5 -> x0, matrix products: 6.11 us -> none  [the longest x3 3.95 us: on_device(): basis_t = jax.scipy.linalg.solve_triangular(lower, sketch.T, lower=True)]
    another operation x9 -> x0, local copies, waits for them, and re-layouts: 5.25 us -> none
  transfers between devices with their start and end apart: 3 -> 0, of which waited for: 3 -> 0; matrix products, arithmetic and copies ran while one was open for 1% -> 0% of each run, Pallas kernels for 0% -> 0%
where the time goes in v2:
time: 81 us; the launch traced here: 80.9 us
  Pallas kernels  80.1 us (99%)
    pallas_call x1, Pallas kernels, main(): pl.pallas_call(functools.partial(main_kernel, nr, scale), out_shape=(jax....  76.5 us
    pallas_call x1, Pallas kernels, finish(): pl.pallas_call(finish_kernel, out_shape=(jax.ShapeDtypeStruct(b.shape, F3...  3.59 us

profile of v2, /device:TPU:1, one launch (start us, length us, event | category | flops | bytes accessed | tf_op | source)
XLA Modules:
  0.0 80.9 jit_solution(12784043663524067631)
XLA Ops:
  0.6 76.5 %sketch_gram_projection.1 = (f32[2048,256]{1,0:T(8,128)}, f32[256,256]{1,0:T(8,128)}, f32[2,16,8,8,128]{4,3,2,1,0:T(8,128)}) custom-call(f32[2048,1024]{1,0:T(8,128)} %refs_0_.1, f32[1024,256]{1,0:T(8,128)} %refs_1_.1), custom_call_target="tpu_custom_call" | custom-call | tf_op jit(solution)/shard_map/sketch_gram_projection/pallas_call | solution.py:409
  77.2 3.6 %coefficients.1 = (f32[2048,256]{1,0:T(8,128)}, f32[256,1024]{1,0:T(8,128)}) custom-call(f32[2048,256]{1,0:T(8,128)} %get-tuple-element.5.b_hbm, f32[256,256]{1,0:T(8,128)} %get-tuple-element.6.x_hbm, f32[2,16,8,8,128]{4,3,2,1,0:T(8,128)} %get-tuple-element.7.c_hbm), custom_call_target="tpu_custom_call" | custom-call | tf_op jit(solution)/shard_map/coefficients/pallas_call | solution.py:475

commit v3 on v2

--- a/solution.py
+++ b/solution.py
@@ -12,24 +12,22 @@
 BF16 = jnp.bfloat16
 MESH = pl.DeviceIdType.MESH
 NF = 8
-CHUNKS = (128, 96, 32)
+CHUNKS = (128, 128)
 
 PLAN = (
-    ("S", 0), ("N", 0), ("R", 0, 0), ("R", 1, 0), ("R", 2, 0), ("S", 1), ("R", 0, 1), ("R", 1, 1), ("R", 2, 1),
-    ("S", 2), ("S", 3), ("S", 4), ("S", 5), ("S", 6), ("R", 0, 2), ("S", 7), ("R", 1, 2), ("R", 2, 2), ("N", 1),
-    ("R", 0, 3), ("R", 1, 3), ("R", 2, 3), ("N", 2), ("R", 0, 4), ("R", 1, 4), ("R", 2, 4), ("N", 3), ("R", 0, 5),
-    ("R", 1, 5), ("R", 2, 5), ("N", 4), ("R", 0, 6), ("R", 1, 6), ("R", 2, 6), ("R", 0, 7), ("R", 1, 7), ("R", 2, 7),
-    ("R", 0, 8), ("A", 0, 0), ("A", 0, 1), ("P", 0, 0), ("R", 1, 8), ("A", 1, 0), ("A", 1, 1), ("P", 0, 1),
-    ("R", 2, 8), ("G", 0), ("P", 0, 2), ("A", 0, 2), ("A", 0, 3), ("P", -1, 0), ("P", 1, 0), ("A", 1, 2), ("A", 2, 0),
-    ("A", 1, 3), ("P", -1, 1), ("P", 1, 1), ("A", 0, 4), ("G", 1), ("A", 0, 5), ("A", 2, 1), ("P", -2, 0),
-    ("P", 2, 0), ("A", 1, 4), ("A", 2, 2), ("A", 0, 6), ("A", 1, 5), ("P", -2, 1), ("P", 2, 1), ("A", 0, 7),
-    ("P", -3, 0), ("A", 2, 3), ("G", 2), ("P", 3, 0), ("P", -1, 2), ("A", 1, 6), ("P", 1, 2), ("A", 2, 4),
-    ("A", 0, 8), ("P", 4, 0), ("C", 0, 0), ("A", 1, 7), ("P", -3, 1), ("A", 2, 5), ("P", 3, 1), ("P", -2, 2),
-    ("C", 0, 1), ("P", 2, 2), ("A", 1, 8), ("P", 4, 1), ("A", 2, 6), ("C", 1, 0), ("C", 1, 1), ("G", 3), ("A", 2, 7),
-    ("P", -3, 2), ("P", 3, 2), ("H", 0, 0), ("A", 2, 8), ("P", 4, 2), ("C", 2, 0), ("H", 0, 1), ("C", 2, 1),
-    ("H", 1, 0), ("C", 0, 2), ("H", 1, 1), ("C", 1, 2), ("H", 2, 0), ("H", 2, 1), ("C", 2, 2), ("H", 3, 0),
-    ("H", 3, 1), ("B", 0), ("C", 0, 3), ("B", 1), ("B", 2), ("B", 3), ("B", 4), ("B", 5), ("B", 6), ("D", 0),
-    ("C", 1, 3), ("B", 7), ("C", 2, 3), ("D", 1), ("D", 2),
+    ("S", 0), ("N", 0), ("R", 0, 0), ("R", 1, 0), ("S", 1), ("R", 0, 1), ("R", 1, 1), ("S", 2), ("S", 3), ("S", 4),
+    ("S", 5), ("R", 0, 2), ("S", 6), ("R", 1, 2), ("N", 1), ("S", 7), ("R", 0, 3), ("R", 1, 3), ("N", 2), ("R", 0, 4),
+    ("R", 1, 4), ("N", 3), ("R", 0, 5), ("R", 1, 5), ("N", 4), ("R", 0, 6), ("R", 1, 6), ("R", 0, 7), ("R", 1, 7),
+    ("R", 0, 8), ("A", 0, 0), ("A", 0, 1), ("P", 0, 0), ("R", 1, 8), ("A", 1, 0), ("G", 0), ("P", 0, 1), ("T", 0),
+    ("A", 0, 2), ("A", 1, 1), ("A", 0, 3), ("P", -1, 0), ("P", 1, 0), ("A", 1, 2), ("A", 0, 4), ("G", 1), ("A", 1, 3),
+    ("P", -1, 1), ("P", 1, 1), ("T", -1), ("T", 1), ("A", 0, 5), ("P", -2, 0), ("P", 2, 0), ("A", 1, 4), ("A", 0, 6),
+    ("G", 2), ("A", 1, 5), ("P", -2, 1), ("P", 2, 1), ("T", -2), ("T", 2), ("A", 0, 7), ("P", -3, 0), ("P", 3, 0),
+    ("A", 1, 6), ("A", 0, 8), ("P", 4, 0), ("C", 0, 0), ("A", 1, 7), ("P", -3, 1), ("P", 3, 1), ("C", 0, 1), ("G", 3),
+    ("T", -3), ("T", 3), ("A", 1, 8), ("P", 4, 1), ("C", 1, 0), ("T", 4), ("H", 0, 0), ("H", 0, 1), ("C", 1, 1),
+    ("H", 0, 2), ("H", 0, 3), ("H", 1, 0), ("H", 1, 1), ("H", 1, 2), ("H", 1, 3), ("C", 0, 2), ("H", 2, 0),
+    ("H", 2, 1), ("H", 2, 2), ("H", 2, 3), ("C", 1, 2), ("H", 3, 0), ("H", 3, 1), ("H", 3, 2), ("H", 3, 3), ("B", 0),
+    ("B", 1), ("B", 2), ("B", 3), ("B", 4), ("C", 0, 3), ("B", 5), ("B", 6), ("B", 7), ("D", 0), ("C", 1, 3),
+    ("D", 1),
 )
 
 
@@ -102,11 +100,11 @@
     ux[lo:hi, 256 + lo : 256 + hi] = w
 
 
-def cholesky_step(p, half, g, ux, win, m):
-    if half == 0:
+def cholesky_step(p, quarter, g, ux, win, m):
+    if quarter == 0:
         panel_begin(p, g, ux, win, m)
-    eliminate(m, range(4 * half, 4 * half + 4))
-    if half == 1:
+    eliminate(m, range(2 * quarter, 2 * quarter + 2))
+    if quarter == 3:
         panel_end(p, ux, win, m)
 
 
@@ -114,9 +112,9 @@
     a_hbm, w_hbm, b_out, x_out, c_out = refs[:5]
     a, a_hi, a_lo, w, w_hi, w_lo, part, rs_buf, st = refs[5:14]
     g_part, g_in, g_sum, gz, g, ux, win, m = refs[14:22]
-    c_part, c_pair, c_half, c_in, c_all = refs[22:27]
-    a_sem, w_sem, rs_s, rs_r, ag_s, ag_r, g1_s, g1_r, gz_s, gz_r, g2_s, g2_r = refs[27:39]
-    cp_s, cp_r, c1_s, c1_r, c2_s, c2_r, cf_s, cf_r, out_sem, near = refs[39:]
+    c_part, c_pair, c_half, c_in, c_all, s_hi, s_lo = refs[22:29]
+    a_sem, w_sem, rs_s, rs_r, ag_s, ag_r, g1_s, g1_r, gz_s, gz_r, g2_s, g2_r = refs[29:41]
+    cp_s, cp_r, c1_s, c1_r, c2_s, c2_r, cf_s, cf_r, out_sem, near = refs[41:]
     row, z = lax.axis_index("row"), lax.axis_index("frame")
     right, left = lax.rem(z + 1, NF), lax.rem(z + NF - 1, NF)
     core, chip = lax.rem(row, 2), lax.div(row, 2)
@@ -153,6 +151,15 @@
     neighbours = ({"frame": right}, {"frame": left}, {"row": mate})
     neighbours += (at_chip(y, x + 1), at_chip(y, x - 1), at_chip(y + 1, x), at_chip(y - 1, x))
 
+    far = lambda o: min(o[0], ny - o[0]) + min(o[1], nx - o[1])
+    steps_to = sorted(((dy, dx) for dy in range(ny) for dx in range(nx)), key=lambda o: (-far(o), o))
+    chip_at = lambda o: lax.rem(y + o[0], ny) * nx + lax.rem(x + o[1], nx)
+    both_cores = [(o, flip) for o in steps_to for flip in (0, 1)][:-2] + [((0, 0), 1)]
+
+    def plane_peer(k):
+        o, flip = both_cores[k - 1]
+        return 2 * chip_at(o) + (1 - core if flip else core)
+
     def greet(which):
         for peer in neighbours:
             pl.semaphore_signal(which, inc=1, device_id=peer, device_id_type=MESH)
@@ -197,11 +204,17 @@
     def sketch(i):
         if i + 3 < 8:
             fetch(i + 3)
-        for side, u in enumerate(units(i)):
+        both = units(i)
+        for side, u in enumerate(both):
             load(u, side, i).wait()
-            hi, lo = split(a[rows_of(u), :])
-            a_hi[rows_of(u), :], a_lo[rows_of(u), :] = hi, lo
-            part[u] = (mm(hi, w_hi[...]) + mm(lo, w_hi[...]) + mm(hi, w_lo[...])).T
+        hi, lo = split(jnp.concatenate([a[rows_of(u), :] for u in both], axis=0))
+        for side, u in enumerate(both):
+            held = slice(side * hb, (side + 1) * hb)
+            a_hi[rows_of(u), :], a_lo[rows_of(u), :] = hi[held], lo[held]
+        halves = mm(jnp.concatenate([hi, lo], axis=0), w_hi[...])
+        total = halves[: 2 * hb] + halves[2 * hb :] + mm(hi, w_lo[...])
+        for side, u in enumerate(both):
+            part[u] = total[side * hb : (side + 1) * hb].T
 
     def rs_copy(side, c, i, u):
         dst = rs_buf.at[side, i, cut(c)]
@@ -233,12 +246,12 @@
                 ag_copy(side, c, j).start()
 
     def g1(k):
-        peer = lax.rem(row + k, nr)
+        peer = plane_peer(k)
         return to_row(g_part.at[at(peer, 8)], g_in.at[k], g1_s, g1_r, peer)
 
     def g2(k):
         piece = g.at[at(row, 8)]
-        return to_row(piece, piece, g2_s, g2_r, lax.rem(row + k, nr))
+        return to_row(piece, piece, g2_s, g2_r, plane_peer(k))
 
     def gzc(k):
         return to_z(g_sum, gz.at[z], gz_s, gz_r, lax.rem(z + k, NF))
@@ -267,7 +280,8 @@
         if stage == 0:
             mine = jnp.concatenate([st[2 * z], st[2 * z + 1]], axis=1)
             g_part[...] = outer(mine, mine, HIGHEST)
-            loop(1, nr, lambda k: g1(k).start())
+            for k in range(1, nr):
+                g1(k).start()
         elif stage == 1:
             g1_all().wait_recv()
             total = g_part[at(row, 8), :]
@@ -275,14 +289,16 @@
                 total = total + g_in[k]
             g_sum[...] = total
             gz[z] = total
-            loop(1, NF, lambda k: gzc(k).start())
+            for k in (4, 3, 5, 2, 6, 1, 7):
+                gzc(k).start()
         elif stage == 2:
             gz_all().wait_recv()
             total = gz[0]
             for k in range(1, NF):
                 total = total + gz[k]
             g[at(row, 8), :] = total
-            loop(1, nr, lambda k: g2(k).start())
+            for k in range(1, nr):
+                g2(k).start()
         else:
             g2_all().wait_recv()
 
@@ -301,12 +317,12 @@
         return to_row(src, c_pair.at[pl.ds(starts[c] // 2, kh)], cp_s.at[c], cp_r.at[c], mate)
 
     def c1(c, k):
-        peer = lax.rem(chip + k, nc)
+        peer = chip_at(steps_to[k - 1])
         return to_row(c_half.at[peer, slots[c]], c_in.at[k, slots[c]], c1_s.at[c], c1_r.at[c], peer * 2 + core)
 
     def c2(c, k):
         piece = c_all.at[core, chip, slots[c]]
-        return to_row(piece, piece, c2_s.at[c], c2_r.at[c], lax.rem(chip + k, nc) * 2 + core)
+        return to_row(piece, piece, c2_s.at[c], c2_r.at[c], chip_at(steps_to[k - 1]) * 2 + core)
 
     def back(c):
         ref = c_all.at[core, :, slots[c]]
@@ -324,14 +340,16 @@
                 r, l = divmod(t, across)
                 i, s = divmod(t, tiles[c])
                 c_half[i, sum(tiles[:c]) + s] = held[8 * r : 8 * r + 8, 128 * l : 128 * l + 128]
-            loop(1, nc, lambda k: c1(c, k).start())
+            for k in range(1, nc):
+                c1(c, k).start()
         elif stage == 2:
             c1_all(c).wait_recv()
             total = c_half[chip, slots[c]]
             for k in range(1, nc):
                 total = total + c_in[k, slots[c]]
             c_all[core, chip, slots[c]] = total
-            loop(1, nc, lambda k: c2(c, k).start())
+            for k in range(1, nc):
+                c2(c, k).start()
         else:
             c2_all(c).wait_recv()
             back(c).start()
@@ -352,11 +370,16 @@
         rows = pl.ds(2 * hb * i, 2 * hb)
         return pltpu.make_async_copy(a.at[rows, pl.ds(0, ux.shape[0])], b_out.at[rows], out_sem.at[len(CHUNKS) + 1 + i])
 
+    def turn(d):
+        block = ahead(d)
+        rows = at(block, 2 * hb)
+        s_hi[rows, :], s_lo[rows, :] = split(jnp.concatenate([st[2 * block].T, st[2 * block + 1].T], axis=0))
+
     def basis_step(i):
         if i == 0:
             x_copy.start()
             held_x.extend(split(ux[:, 256:512]))
-        hi, lo = split(jnp.concatenate([st[2 * i].T, st[2 * i + 1].T], axis=0))
+        hi, lo = (ref[2 * hb * i : 2 * hb * (i + 1), :] for ref in (s_hi, s_lo))
         block = outer(hi, held_x[0]) + outer(lo, held_x[0]) + outer(hi, held_x[1])
         a[2 * hb * i : 2 * hb * (i + 1), 0 : ux.shape[0]] = block * scale
         b_copy(i).start()
@@ -371,6 +394,7 @@
         "C": plane_step,
         "D": c_land,
         "H": functools.partial(cholesky_step, g=g, ux=ux, win=win, m=m),
+        "T": turn,
         "B": basis_step,
     }
     for name, *numbers in PLAN:
@@ -422,6 +446,7 @@
             vm(k, k), vm(nr, 8, k), vm(8, k), vm(NF, 8, k), vm(k, k),
             vm(k, 2 * k), vm(64, k), vm(64, 128),
             vm(k, frames), vm(k // 2, frames), vm(nc, tiles, 8, 128), vm(nc, tiles, 8, 128), vm(2, nc, tiles, 8, 128),
+            vb(rows, k), vb(rows, k),
             sem(2, 8), one, sem(2), sem(2, nq, 7), sem(2), sem(2, nq, 7),
             one, one, one, one, one, one,
             sem(nq), sem(nq), sem(nq), sem(nq), sem(nq), sem(nq), sem(nq), sem(nq), sem(nq + 1 + NF),
@@ -462,9 +487,13 @@
                 place = (sum(CHUNKS[:q]) + h * n // 2) // 8 + r
                 lines[place] = jnp.concatenate([c[h, i, first + t] for i, t in line], axis=1)
     c_hi, c_lo = split(jnp.concatenate(lines, axis=0))
-    coef[...] = mm(x_hi, c_hi) + mm(x_lo, c_hi) + mm(x_hi, c_lo)
-    stores.append(pltpu.make_async_copy(coef, coef_hbm, f_sem))
-    stores[-1].start()
+    wide = coef.shape[1] // 2
+    for i in range(2):
+        cols = pl.ds(i * wide, wide)
+        hi, lo = (v[:, i * wide : (i + 1) * wide] for v in (c_hi, c_lo))
+        coef[:, cols] = mm(x_hi, hi) + mm(x_lo, hi) + mm(x_hi, lo)
+        stores.append(pltpu.make_async_copy(coef.at[:, cols], coef_hbm.at[:, cols], f_sem.at[i]))
+        stores[-1].start()
     for copy in stores:
         copy.wait()
 
@@ -479,7 +508,7 @@
         out_specs=[hbm] * 2,
         scratch_shapes=[
             vm(*b.shape), vm(*x.shape), vm(*c.shape), vm(x.shape[0], frames),
-            pltpu.SemaphoreType.DMA((4,)), pltpu.SemaphoreType.DMA((4,)), pltpu.SemaphoreType.DMA((2,)), pltpu.SemaphoreType.DMA,
+            pltpu.SemaphoreType.DMA((4,)), pltpu.SemaphoreType.DMA((4,)), pltpu.SemaphoreType.DMA((2,)), pltpu.SemaphoreType.DMA((2,)),
         ],
         compiler_params=pltpu.CompilerParams(vmem_limit_bytes=62 * 1024 * 1024),
         name="coefficients",

time: 81 us -> 77 us (0.951)
  Pallas kernels: 80.1 us -> 76.1 us
    pallas_call x1, Pallas kernels: 76.5 us -> 72.7 us  [main(): pl.pallas_call(functools.partial(main_kernel, nr, scale), out_shape=(jax....]
where the time goes in v3:
time: 77 us; the launch traced here: 76.9 us
  Pallas kernels  76.1 us (99%)
  between operations  0.8 us (1%)
    pallas_call x1, Pallas kernels, main(): pl.pallas_call(functools.partial(main_kernel, nr, scale), out_shape=(jax....  72.7 us
    pallas_call x1, Pallas kernels, finish(): pl.pallas_call(finish_kernel, out_shape=(jax.ShapeDtypeStruct(b.shape, F3...  3.44 us

profile of v3, /device:TPU:1, one launch (start us, length us, event | category | flops | bytes accessed | tf_op | source)
XLA Modules:
  0.0 76.9 jit_solution(835402532383188824)
XLA Ops:
  0.6 72.7 %sketch_gram_projection.1 = (f32[2048,256]{1,0:T(8,128)}, f32[256,256]{1,0:T(8,128)}, f32[2,16,8,8,128]{4,3,2,1,0:T(8,128)}) custom-call(f32[2048,1024]{1,0:T(8,128)} %refs_0_.1, f32[1024,256]{1,0:T(8,128)} %refs_1_.1), custom_call_target="tpu_custom_call" | custom-call | tf_op jit(solution)/shard_map/sketch_gram_projection/pallas_call | solution.py:433
  73.3 3.4 %coefficients.1 = (f32[2048,256]{1,0:T(8,128)}, f32[256,1024]{1,0:T(8,128)}) custom-call(f32[2048,256]{1,0:T(8,128)} %get-tuple-element.5.b_hbm, f32[256,256]{1,0:T(8,128)} %get-tuple-element.6.x_hbm, f32[2,16,8,8,128]{4,3,2,1,0:T(8,128)} %get-tuple-element.7.c_hbm), custom_call_target="tpu_custom_call" | custom-call | tf_op jit(solution)/shard_map/coefficients/pallas_call | solution.py:504

commit v4 on v3

--- a/solution.py
+++ b/solution.py
@@ -12,22 +12,27 @@
 BF16 = jnp.bfloat16
 MESH = pl.DeviceIdType.MESH
 NF = 8
-CHUNKS = (128, 128)
+CHUNKS = (96, 96, 64)
+CUTS = (96, 96, 64)
 
 PLAN = (
-    ("S", 0), ("N", 0), ("R", 0, 0), ("R", 1, 0), ("S", 1), ("R", 0, 1), ("R", 1, 1), ("S", 2), ("S", 3), ("S", 4),
-    ("S", 5), ("R", 0, 2), ("S", 6), ("R", 1, 2), ("N", 1), ("S", 7), ("R", 0, 3), ("R", 1, 3), ("N", 2), ("R", 0, 4),
-    ("R", 1, 4), ("N", 3), ("R", 0, 5), ("R", 1, 5), ("N", 4), ("R", 0, 6), ("R", 1, 6), ("R", 0, 7), ("R", 1, 7),
-    ("R", 0, 8), ("A", 0, 0), ("A", 0, 1), ("P", 0, 0), ("R", 1, 8), ("A", 1, 0), ("G", 0), ("P", 0, 1), ("T", 0),
-    ("A", 0, 2), ("A", 1, 1), ("A", 0, 3), ("P", -1, 0), ("P", 1, 0), ("A", 1, 2), ("A", 0, 4), ("G", 1), ("A", 1, 3),
-    ("P", -1, 1), ("P", 1, 1), ("T", -1), ("T", 1), ("A", 0, 5), ("P", -2, 0), ("P", 2, 0), ("A", 1, 4), ("A", 0, 6),
-    ("G", 2), ("A", 1, 5), ("P", -2, 1), ("P", 2, 1), ("T", -2), ("T", 2), ("A", 0, 7), ("P", -3, 0), ("P", 3, 0),
-    ("A", 1, 6), ("A", 0, 8), ("P", 4, 0), ("C", 0, 0), ("A", 1, 7), ("P", -3, 1), ("P", 3, 1), ("C", 0, 1), ("G", 3),
-    ("T", -3), ("T", 3), ("A", 1, 8), ("P", 4, 1), ("C", 1, 0), ("T", 4), ("H", 0, 0), ("H", 0, 1), ("C", 1, 1),
-    ("H", 0, 2), ("H", 0, 3), ("H", 1, 0), ("H", 1, 1), ("H", 1, 2), ("H", 1, 3), ("C", 0, 2), ("H", 2, 0),
-    ("H", 2, 1), ("H", 2, 2), ("H", 2, 3), ("C", 1, 2), ("H", 3, 0), ("H", 3, 1), ("H", 3, 2), ("H", 3, 3), ("B", 0),
-    ("B", 1), ("B", 2), ("B", 3), ("B", 4), ("C", 0, 3), ("B", 5), ("B", 6), ("B", 7), ("D", 0), ("C", 1, 3),
-    ("D", 1),
+    ("S", 0), ("N", 0), ("R", 0, 0), ("R", 1, 0), ("R", 2, 0), ("S", 1), ("R", 0, 1), ("R", 1, 1), ("R", 2, 1),
+    ("S", 2), ("S", 3), ("S", 4), ("R", 0, 2), ("S", 5), ("R", 1, 2), ("S", 6), ("R", 2, 2), ("N", 1), ("S", 7),
+    ("R", 0, 3), ("R", 1, 3), ("R", 2, 3), ("N", 2), ("R", 0, 4), ("R", 1, 4), ("R", 2, 4), ("N", 3), ("R", 0, 5),
+    ("R", 1, 5), ("R", 2, 5), ("N", 4), ("R", 0, 6), ("R", 1, 6), ("R", 2, 6), ("R", 0, 7), ("R", 1, 7), ("R", 2, 7),
+    ("R", 0, 8), ("A", 0, 0), ("A", 0, 1), ("P", 0, 0, 96), ("R", 1, 8), ("A", 1, 0), ("A", 1, 1), ("P", 0, 96, 96),
+    ("R", 2, 8), ("G", 0), ("P", 0, 192, 64), ("T", 0), ("A", 0, 2), ("A", 0, 3), ("P", -1, 0, 96), ("P", 1, 0, 96),
+    ("A", 1, 2), ("A", 2, 0), ("A", 0, 4), ("A", 0, 5), ("A", 1, 3), ("A", 2, 1), ("G", 1), ("P", -2, 0, 96),
+    ("P", 2, 0, 96), ("P", -1, 96, 96), ("P", 1, 96, 96), ("A", 0, 6), ("A", 1, 4), ("A", 2, 2), ("A", 0, 7),
+    ("P", -3, 0, 96), ("P", 3, 0, 96), ("A", 1, 5), ("P", -2, 96, 96), ("P", 2, 96, 96), ("A", 2, 3),
+    ("P", -1, 192, 64), ("P", 1, 192, 64), ("G", 2), ("T", -1), ("A", 0, 8), ("P", 4, 0, 96), ("C", 0, 0), ("T", 1),
+    ("A", 1, 6), ("A", 2, 4), ("C", 0, 1), ("A", 1, 7), ("P", -3, 96, 96), ("P", 3, 96, 96), ("A", 2, 5),
+    ("P", -2, 192, 64), ("P", 2, 192, 64), ("T", -2), ("T", 2), ("A", 1, 8), ("P", 4, 96, 96), ("C", 1, 0),
+    ("A", 2, 6), ("G", 3), ("H", 0, 0), ("C", 1, 1), ("A", 2, 7), ("P", -3, 192, 64), ("P", 3, 192, 64), ("T", -3),
+    ("C", 0, 2), ("A", 2, 8), ("P", 4, 192, 64), ("C", 2, 0), ("T", 3), ("T", 4), ("H", 0, 1), ("C", 2, 1),
+    ("H", 1, 0), ("H", 1, 1), ("H", 2, 0), ("C", 1, 2), ("H", 2, 1), ("H", 3, 0), ("C", 0, 3), ("H", 3, 1),
+    ("C", 2, 2), ("D", 0), ("B", 0), ("B", 1), ("B", 2), ("B", 3), ("B", 4), ("B", 5), ("B", 6), ("B", 7),
+    ("C", 1, 3), ("D", 1), ("C", 2, 3), ("D", 2),
 )
 
 
@@ -72,8 +77,13 @@
     lanes = lambda x, k: jnp.broadcast_to(x[:, k : k + 1], (8, 128))
     subl = lambda x, k: jnp.broadcast_to(x[k : k + 1, :], (8, 128))
     tiles = {i: m[8 * i : 8 * i + 8, :] for i in range(groups[0], 8)}
+    own = [lanes(tiles[groups[0]], 8 * groups[0] + k) for k in range(8)]
     for t in groups:
-        cols = {i: [lanes(tiles[i], 8 * t + k) for k in range(8)] for i in range(t, 8)}
+        cols = {i: [lanes(tiles[i], 8 * t + k) for k in range(8)] for i in range(t + 1, 8)}
+        cols[t] = own
+        more = t + 1 in groups
+        if more:
+            own = [lanes(tiles[t + 1], 8 * t + 8 + k) for k in range(8)]
         pivots = jnp.ones((8, 128), F32)
         for k in range(8):
             row = subl(tiles[t], k)
@@ -85,6 +95,8 @@
                 mult = cols[i][k] * inv
                 if i == t:
                     mult = jnp.where(sub > k, mult, 0.0)
+                if more and i == t + 1:
+                    own = [own[j] - mult * subl(cols[i][k], j) for j in range(8)]
                 tiles[i] = tiles[i] - mult * row
                 for j in range(k + 1, 8):
                     cols[i][j] = cols[i][j] - mult * ahead[j]
@@ -100,11 +112,11 @@
     ux[lo:hi, 256 + lo : 256 + hi] = w
 
 
-def cholesky_step(p, quarter, g, ux, win, m):
-    if quarter == 0:
+def cholesky_step(p, half, g, ux, win, m):
+    if half == 0:
         panel_begin(p, g, ux, win, m)
-    eliminate(m, range(2 * quarter, 2 * quarter + 2))
-    if quarter == 3:
+    eliminate(m, range(4 * half, 4 * half + 4))
+    if half == 1:
         panel_end(p, ux, win, m)
 
 
@@ -128,8 +140,9 @@
     starts = [sum(CHUNKS[:c]) for c in range(len(CHUNKS))]
     span = [slice(starts[c], starts[c] + CHUNKS[c]) for c in range(len(CHUNKS))]
     cut = lambda c: pl.ds(starts[c], CHUNKS[c])
-    tiles = [n * across // 16 // nc for n in CHUNKS]
-    slots = [pl.ds(sum(tiles[:c]), tiles[c]) for c in range(len(CHUNKS))]
+    firsts = [sum(CUTS[:c]) for c in range(len(CUTS))]
+    tiles = [n * across // 16 // nc for n in CUTS]
+    slots = [pl.ds(sum(tiles[:c]), tiles[c]) for c in range(len(CUTS))]
 
     def to_z(src, dst, s, r, peer):
         return pltpu.make_async_remote_copy(src, dst, s, r, device_id={"frame": peer}, device_id_type=MESH)
@@ -302,19 +315,19 @@
         else:
             g2_all().wait_recv()
 
-    def project(d, c):
+    def project(d, first, n):
         block = ahead(d)
-        kc = CHUNKS[c]
+        cols = slice(first, first + n)
         rows = at(block, 2 * hb)
-        hi, lo = split(jnp.concatenate([st[2 * block, span[c]], st[2 * block + 1, span[c]]], axis=1))
+        hi, lo = split(jnp.concatenate([st[2 * block, cols], st[2 * block + 1, cols]], axis=1))
         both = mm(jnp.concatenate([hi, lo], 0), a_hi[rows, :])
-        total = both[:kc] + both[kc:] + mm(hi, a_lo[rows, :])
-        c_part[span[c], :] = total if d == 0 else c_part[span[c], :] + total
+        total = both[:n] + both[n:] + mm(hi, a_lo[rows, :])
+        c_part[cols, :] = total if d == 0 else c_part[cols, :] + total
 
     def pair(c):
-        kh = CHUNKS[c] // 2
-        src = c_part.at[pl.ds(pl.multiple_of(starts[c] + (1 - core) * kh, 8), kh)]
-        return to_row(src, c_pair.at[pl.ds(starts[c] // 2, kh)], cp_s.at[c], cp_r.at[c], mate)
+        kh = CUTS[c] // 2
+        src = c_part.at[pl.ds(pl.multiple_of(firsts[c] + (1 - core) * kh, 8), kh)]
+        return to_row(src, c_pair.at[pl.ds(firsts[c] // 2, kh)], cp_s.at[c], cp_r.at[c], mate)
 
     def c1(c, k):
         peer = chip_at(steps_to[k - 1])
@@ -329,13 +342,13 @@
         return to_row(ref, ref, cf_s.at[c], cf_r.at[c], mate)
 
     def plane_step(c, stage):
-        kh = CHUNKS[c] // 2
+        kh = CUTS[c] // 2
         if stage == 0:
             pair(c).start()
         elif stage == 1:
             pair(c).wait_recv()
-            mine = pl.ds(pl.multiple_of(starts[c] + core * kh, 8), kh)
-            held = c_part[mine, :] + c_pair[starts[c] // 2 : starts[c] // 2 + kh]
+            mine = pl.ds(pl.multiple_of(firsts[c] + core * kh, 8), kh)
+            held = c_part[mine, :] + c_pair[firsts[c] // 2 : firsts[c] // 2 + kh]
             for t in range(kh // 8 * across):
                 r, l = divmod(t, across)
                 i, s = divmod(t, tiles[c])
@@ -363,12 +376,12 @@
         for h in range(2):
             c_copy(c, h).start()
 
-    x_copy = pltpu.make_async_copy(ux.at[:, 256:512], x_out, out_sem.at[len(CHUNKS)])
+    x_copy = pltpu.make_async_copy(ux.at[:, 256:512], x_out, out_sem.at[len(CUTS)])
     held_x = []
 
     def b_copy(i):
         rows = pl.ds(2 * hb * i, 2 * hb)
-        return pltpu.make_async_copy(a.at[rows, pl.ds(0, ux.shape[0])], b_out.at[rows], out_sem.at[len(CHUNKS) + 1 + i])
+        return pltpu.make_async_copy(a.at[rows, pl.ds(0, ux.shape[0])], b_out.at[rows], out_sem.at[len(CUTS) + 1 + i])
 
     def turn(d):
         block = ahead(d)
@@ -400,7 +413,7 @@
     for name, *numbers in PLAN:
         steps[name](*numbers)
 
-    for c in range(len(CHUNKS)):
+    for c in range(len(CUTS)):
         pair(c).wait_send()
         back(c).wait_send()
         c1_all(c).wait_send()
@@ -415,7 +428,7 @@
     x_copy.wait()
     for i in range(NF):
         b_copy(i).wait()
-    for c in range(len(CHUNKS)):
+    for c in range(len(CUTS)):
         for h in range(2):
             c_copy(c, h).wait()
 
@@ -423,7 +436,7 @@
 def main(snapshots, test_matrix, nr, scale):
     rows, frames = snapshots.shape
     k = test_matrix.shape[1]
-    hb, nc, nq = rows // NF // 2, nr // 2, len(CHUNKS)
+    hb, nc, nq, ncut = rows // NF // 2, nr // 2, len(CHUNKS), len(CUTS)
     tiles = k * (frames // 128) // 16 // nc
     hbm = pl.BlockSpec(memory_space=pltpu.HBM)
     vm = lambda *shape: pltpu.VMEM(shape, F32)
@@ -449,7 +462,7 @@
             vb(rows, k), vb(rows, k),
             sem(2, 8), one, sem(2), sem(2, nq, 7), sem(2), sem(2, nq, 7),
             one, one, one, one, one, one,
-            sem(nq), sem(nq), sem(nq), sem(nq), sem(nq), sem(nq), sem(nq), sem(nq), sem(nq + 1 + NF),
+            sem(ncut), sem(ncut), sem(ncut), sem(ncut), sem(ncut), sem(ncut), sem(ncut), sem(ncut), sem(ncut + 1 + NF),
             pltpu.SemaphoreType.REGULAR((4,)),
         ],
         compiler_params=pltpu.CompilerParams(
@@ -480,11 +493,11 @@
     across = coef.shape[1] // 128
     lines = [None] * (x.shape[0] // 8)
     for h in range(2):
-        for q, n in enumerate(CHUNKS):
-            first, tiles = sum(CHUNKS[:q]) * total // x.shape[0], n * total // x.shape[0]
+        for q, n in enumerate(CUTS):
+            first, tiles = sum(CUTS[:q]) * total // x.shape[0], n * total // x.shape[0]
             for r in range(n // 16):
                 line = [divmod(r * across + l, tiles) for l in range(across)]
-                place = (sum(CHUNKS[:q]) + h * n // 2) // 8 + r
+                place = (sum(CUTS[:q]) + h * n // 2) // 8 + r
                 lines[place] = jnp.concatenate([c[h, i, first + t] for i, t in line], axis=1)
     c_hi, c_lo = split(jnp.concatenate(lines, axis=0))
     wide = coef.shape[1] // 2

time: 77 us -> 76.9 us (level)
  no operation moved by 1% of the time
where the time goes in v4:
time: 76.9 us; the launch traced here: 76.8 us
  Pallas kernels  76 us (99%)
  between operations  0.8 us (1%)
    pallas_call x1, Pallas kernels, main(): pl.pallas_call(functools.partial(main_kernel, nr, scale), out_shape=(jax....  72.6 us
    pallas_call x1, Pallas kernels, finish(): pl.pallas_call(finish_kernel, out_shape=(jax.ShapeDtypeStruct(b.shape, F3...  3.44 us

profile of v4, /device:TPU:1, one launch (start us, length us, event | category | flops | bytes accessed | tf_op | source)
XLA Modules:
  0.0 76.8 jit_solution(9089933014004469398)
XLA Ops:
  0.6 72.6 %sketch_gram_projection.1 = (f32[2048,256]{1,0:T(8,128)}, f32[256,256]{1,0:T(8,128)}, f32[2,16,8,8,128]{4,3,2,1,0:T(8,128)}) custom-call(f32[2048,1024]{1,0:T(8,128)} %refs_0_.1, f32[1024,256]{1,0:T(8,128)} %refs_1_.1), custom_call_target="tpu_custom_call" | custom-call | tf_op jit(solution)/shard_map/sketch_gram_projection/pallas_call | solution.py:446
  73.2 3.4 %coefficients.1 = (f32[2048,256]{1,0:T(8,128)}, f32[256,1024]{1,0:T(8,128)}) custom-call(f32[2048,256]{1,0:T(8,128)} %get-tuple-element.5.b_hbm, f32[256,256]{1,0:T(8,128)} %get-tuple-element.6.x_hbm, f32[2,16,8,8,128]{4,3,2,1,0:T(8,128)} %get-tuple-element.7.c_hbm), custom_call_target="tpu_custom_call" | custom-call | tf_op jit(solution)/shard_map/coefficients/pallas_call | solution.py:517
